TPU v7x, 256 devices: a whole 4x4x8 slice. The times are simulated.
256 devices in a mesh: row: 16 (over z_lo, y, core), col: 16 (over z_hi, x).
Axes of the slice: x: 4, y: 4, z: 8 (z_hi: 4, z_lo: 2; z = z_hi * 2 + z_lo), core: 2. Of those that a mesh axis runs over, the one named last changes fastest.
Arguments:
- inputs: bfloat16 [12288, 4096], P('col'), may hold values from -6 to 6
- cotangent: bfloat16 [12288, 4096], P('col', 'row'), may hold values from -6 to 6
- gate_weight: bfloat16 [4096, 14336], P('col', 'row'), may hold values from -0.09375 to 0.09375
- up_weight: bfloat16 [4096, 14336], P('col', 'row'), may hold values from -0.09375 to 0.09375
- proj_in: bfloat16 [14336, 128], P('row'), may hold values from -0.046875 to 0.046875
- proj_out: bfloat16 [4096, 128], P('row'), may hold values from -0.09375 to 0.09375
- inverse_fisher: bfloat16 [16384, 16384], P('row', 'col'), may hold values from -0.05 to 2.1
- stored: bfloat16 [16384, 16384], P('row', 'col'), may hold values from -0.014953613 to 0.014953613
Outputs:
- scores: float32 [192, 16384], P('col', 'row')
All inputs are finite; a program needn't handle non-finite values.
Results may differ from a plain program's by a relative error of at most 0.005.
Values may be sent and summed in bfloat16 or wider, within the bound.
A program may use at most 256 MiB of HBM per device.

v0:
```python
import jax
import jax.numpy as jnp
from jax import lax
from jax.sharding import PartitionSpec as P

KIN = 128
KOUT = 128
TOK_SEQ = 64


def body(inputs, cotangent, gate_weight, up_weight, proj_in, proj_out, inverse_fisher, stored):
    tokens_here = inputs.shape[0]
    seqs_here = tokens_here // TOK_SEQ
    gate_part = jnp.dot(
        inputs,
        lax.all_gather(gate_weight, "col", axis=0, tiled=True),
        preferred_element_type=jnp.float32,
    )
    up_part = jnp.dot(
        inputs,
        lax.all_gather(up_weight, "col", axis=0, tiled=True),
        preferred_element_type=jnp.float32,
    )
    hidden = (jax.nn.silu(gate_part) * up_part).astype(jnp.bfloat16)
    left_part = jnp.dot(hidden, proj_in, preferred_element_type=jnp.float32)
    right_part = jnp.dot(cotangent, proj_out, preferred_element_type=jnp.float32)
    block_width = inverse_fisher.shape[0]
    left_proj, right_proj = lax.psum((left_part, right_part), "row")
    right_seq = right_proj.reshape(seqs_here, TOK_SEQ, KOUT)
    full_grads = jnp.einsum(
        "sti,stj->sij",
        left_proj.reshape(seqs_here, TOK_SEQ, KIN),
        right_seq,
        precision=lax.Precision.HIGHEST,
    )
    full_grads = full_grads.reshape(seqs_here, KIN * KOUT)
    block_grads = lax.dynamic_slice_in_dim(
        full_grads, lax.axis_index("row") * block_width, block_width, 1
    )
    every_seq = lax.all_gather(block_grads.astype(jnp.bfloat16), "col", axis=0, tiled=True)
    precond_part = jnp.dot(every_seq, inverse_fisher, preferred_element_type=jnp.float32)
    precond = lax.psum(precond_part, "row").astype(jnp.bfloat16)
    return lax.psum_scatter(
        lax.dot_general(
            precond, stored, (((1,), (1,)), ((), ())), preferred_element_type=jnp.float32
        ),
        "col",
        scatter_dimension=0,
        tiled=True,
    )


def solution(mesh):
    return jax.shard_map(
        body,
        mesh=mesh,
        in_specs=(
            P("col", None),
            P("col", "row"),
            P("col", "row"),
            P("col", "row"),
            P("row", None),
            P("row", None),
            P("row", "col"),
            P("row", "col"),
        ),
        out_specs=P("col", "row"),
        check_vma=False,
    )
```

profile of v0, /device:TPU:24, one launch (start us, length us, event | category | flops | bytes accessed | tf_op | source)
XLA Modules:
  0.0 547.6 jit_solution(14486809837716506517)
XLA Ops:
  6.5 0.0 all-gather.4.cloned.1.call-start
  6.5 0.7 all-gather.4.cloned.1.call-update
  7.3 0.0 all-gather.6.cloned.1.call-start
  7.3 0.7 all-gather.6.cloned.1.call-update
  8.0 0.0 all-reduce.6.cloned.1.call-start
  8.1 2.0 fusion.7
  10.0 99.0 %all-gather.4.cloned.1.call-done = bf16[4096,896]{1,0:T(8,128)(2,1)} async-done(((bf16[256,896]{1,0:T(8,128)(2,1)}), bf16[4096,896]{1,0:T(8,128)(2,1)}) %all-gather.4.cloned.1.call-update) | async-done | bytes 7340048 | tf_op jit(solution)/shard_map/all_gather | solution.py:16
  109.1 11.9 %fusion.6 = f32[768,896]{1,0:T(8,128)} fusion(bf16[768,4096]{1,0:T(8,128)(2,1)} %param.8, bf16[4096,896]{1,0:T(8,128)(2,1)} %all-gather.4.cloned.1.call-done), kind=kOutput, calls=%fused_computation.8 | convolution fusion | flops 5637144576 | bytes 16384000 | tf_op jit(solution)/shard_map/dot_general | solution.py:14
  121.0 96.4 %all-gather.6.cloned.1.call-done = bf16[4096,896]{1,0:T(8,128)(2,1)} async-done(((bf16[256,896]{1,0:T(8,128)(2,1)}), bf16[4096,896]{1,0:T(8,128)(2,1)}) %all-gather.6.cloned.1.call-update) | async-done | bytes 7340048 | tf_op jit(solution)/shard_map/all_gather | solution.py:21
  217.5 13.4 %fusion.1 = f32[768,128]{1,0:T(8,128)} fusion(bf16[896,128]{1,0:T(8,128)(2,1)S(1)} %copy-done.2, f32[768,896]{1,0:T(8,128)} %fusion.6, bf16[768,4096]{1,0:T(8,128)(2,1)} %param.8, bf16[4096,896]{1,0:T(8,128)(2,1)} %all-gather.6.cloned.1.call-done), kind=kOutput, calls=%fused_computation.1 | convolution fusion | flops 5817434112 | bytes 17006592 | tf_op jit(solution)/shard_map/dot_general | solution.py:25
  230.9 0.0 all-reduce.6.cloned.1.call-update
  230.9 130.2 %all-reduce.6.cloned.1.call-done = (f32[12,64,128]{2,1,0:T(8,128)}, f32[12,64,128]{2,1,0:T(8,128)}) async-done(((f32[12,64,128]{2,1,0:T(8,128)}, f32[12,64,128]{2,1,0:T(8,128)}), (f32[12,64,128]{2,1,0:T(8,128)}, f32[12,64,128]{2,1,0:T(8,128)})) %all-reduce.6.cloned.1.call-update) | async-done | bytes 786448 | tf_op jit(solution)/shard_map/psum | solution.py:28
  361.1 2.5 fusion.8
  363.7 0.3 copy.9
  364.0 46.5 %all-gather = bf16[16,12,1024]{2,1,0:T(8,128)(2,1)S(1)} all-gather(bf16[1,12,1024]{2,1,0:T(8,128)(2,1)S(1)} %fusion.4), channel_id=1, replica_groups=mesh['row'=16,'col'=16] {'col'}, dimensions={0}, use_global_device_ids=true | all-gather | bytes 417792 | tf_op jit(solution)/shard_map/all_gather | solution.py:40
  410.5 0.1 reshape.13
  410.6 0.6 fusion.9
  411.2 0.0 copy-start.1
  411.2 61.7 %all-reduce.7 = bf16[192,1024]{1,0:T(8,128)(2,1)S(1)} all-reduce(f32[192,1024]{1,0:T(8,128)S(1)} %fusion.9), channel_id=1, replica_groups=mesh['row'=16,'col'=16] {'row'}, use_global_device_ids=true, to_apply=%region_2.3 | all-reduce | flops 196608 | bytes 1179648 | tf_op jit(solution)/shard_map/psum | solution.py:42
  473.0 2.4 fusion.10
  475.4 49.3 %fusion = f32[16,1024]{1,0:T(8,128)S(1)} fusion(f32[192,1024]{1,0:T(8,128)S(1)} %fusion.10), kind=kCustom, calls=%all-reduce-scatter | all-reduce-scatter fusion | flops 262145 | bytes 852992
  524.7 1.3 collective-permute-start.2
  526.0 1.3 collective-permute-start.1
  527.3 3.8 collective-permute-start
  531.1 6.9 %collective-permute-start.3 = (f32[12,1024]{1,0:T(8,128)S(1)}, f32[12,1024]{1,0:T(8,128)S(1)}, u32[]{:S(2)}, u32[]{:S(2)}) collective-permute-start(f32[12,1024]{1,0:T(8,128)S(1)} %slice), channel_id=1, source_target_pairs={{0,4},{1,5},{2,6},{3,7},{4,8},{5,9},{6,10},{7,11},{8,12},{9,13},{1... | collective-permute-start | bytes 147464
  538.0 0.6 dynamic-slice.4
  539.2 0.6 collective-permute-done.3
  539.9 0.0 collective-permute-done.2
  539.9 0.0 collective-permute-done.1
  539.9 0.0 collective-permute-done
  539.9 0.6 concatenate
  540.5 0.6 constant_dynamic-slice_fusion
  (8 shorter events, 0.1 us)
Async XLA Ops:
  6.5 404.1 %copy-start = (bf16[1024,1024]{1,0:T(8,128)(2,1)S(1)}, bf16[1024,1024]{1,0:T(8,128)(2,1)}, u32[]{:S(2)}) copy-start(bf16[1024,1024]{1,0:T(8,128)(2,1)} %param.14) | copy-start | bytes 6291460
  6.5 102.5 %all-gather.4.cloned.1.call-start = ((), (), s32[]{:S(2)}) async-start(), calls=%async_computation | async-start | bytes 7798784 | tf_op jit(solution)/shard_map/all_gather | solution.py:16
  7.3 210.2 %all-gather.6.cloned.1.call-start = ((), (), s32[]{:S(2)}) async-start(), calls=%async_computation.1 | async-start | bytes 7798784 | tf_op jit(solution)/shard_map/all_gather | solution.py:21
  8.0 353.1 %all-reduce.6.cloned.1.call-start = ((), (), s32[]{:S(2)}) async-start(), calls=%async_computation.2 | async-start | bytes 1572864 | tf_op jit(solution)/shard_map/psum | solution.py:28
  10.0 207.4 %copy-start.2 = (bf16[896,128]{1,0:T(8,128)(2,1)S(1)}, bf16[896,128]{1,0:T(8,128)(2,1)}, u32[]{:S(2)}) copy-start(bf16[896,128]{1,0:T(8,128)(2,1)} %param.12) | copy-start | bytes 688132
  411.2 126.8 %copy-start.1 = (u32[256]{0:T(256)S(1)}, u32[256]{0:T(256)}, u32[]{:S(2)}) copy-start(u32[256]{0:T(256)} %constant.16) | copy-start | bytes 3076
  524.7 15.2 %collective-permute-start.2 = (f32[16,1024]{1,0:T(8,128)S(1)}, f32[16,1024]{1,0:T(8,128)S(1)}, u32[]{:S(2)}, u32[]{:S(2)}) collective-permute-start(f32[16,1024]{1,0:T(8,128)S(1)} %fusion), channel_id=1, source_target_pairs={{0,3},{1,4},{2,5},{3,6},{4,7},{5,8},{6,9},{7,10},{8,11},{9,12},{10... | collective-permute-start | bytes 196616
  526.0 13.9 %collective-permute-start.1 = (f32[16,1024]{1,0:T(8,128)S(1)}, f32[16,1024]{1,0:T(8,128)S(1)}, u32[]{:S(2)}, u32[]{:S(2)}) collective-permute-start(f32[16,1024]{1,0:T(8,128)S(1)} %fusion), channel_id=1, source_target_pairs={{0,2},{1,3},{2,4},{3,5},{4,6},{5,7},{6,8},{7,9},{8,10},{9,11},{10,... | collective-permute-start | bytes 196616
  527.3 12.6 %collective-permute-start = (f32[16,1024]{1,0:T(8,128)S(1)}, f32[16,1024]{1,0:T(8,128)S(1)}, u32[]{:S(2)}, u32[]{:S(2)}) collective-permute-start(f32[16,1024]{1,0:T(8,128)S(1)} %fusion), channel_id=1, source_target_pairs={{0,1},{1,2},{2,3},{3,4},{4,5},{5,6},{6,7},{7,8},{8,9},{9,10},{10,1... | collective-permute-start | bytes 196616
  531.1 8.8 %collective-permute-start.3 = (f32[12,1024]{1,0:T(8,128)S(1)}, f32[12,1024]{1,0:T(8,128)S(1)}, u32[]{:S(2)}, u32[]{:S(2)}) collective-permute-start(f32[12,1024]{1,0:T(8,128)S(1)} %slice), channel_id=1, source_target_pairs={{0,4},{1,5},{2,6},{3,7},{4,8},{5,9},{6,10},{7,11},{8,12},{9,13},{1... | collective-permute-start | bytes 147464
Sparse Core Ops, SparseCore 0:
  9.8 99.2 all-gather.3
  111.5 105.8 all-gather.5
  231.0 130.0 all-reduce.5
where the time goes:
time: 550 us; the launch traced here: 548 us
  waiting for transfers between devices  328 us (60%)
  blocking collectives  157 us (29%)
  matrix products  32.9 us (6%)
  between operations  13.9 us (3%)
  starting transfers between devices  13.3 us (2%)
    psum x1, waiting for transfers between devices, body(): left_proj, right_proj = lax.psum((left_part, right_part), 'row')  130 us
    all_gather x1, waiting for transfers between devices, body(): lax.all_gather(gate_weight, 'col', axis=0, tiled=True)  99 us
    all_gather x1, waiting for transfers between devices, body(): lax.all_gather(up_weight, 'col', axis=0, tiled=True)  96.4 us
    psum x1, blocking collectives, body(): precond = lax.psum(precond_part, 'row').astype(jnp.bfloat16)  61.7 us
    unnamed x1, blocking collectives  49.3 us
    all_gather x1, blocking collectives, body(): lax.all_gather(block_grads.astype(jnp.bfloat16), 'col', axis=0, tiled=True)  46.5 us
    dot_general x1, matrix products, body(): left_part = jnp.dot(hidden, proj_in, preferred_element_type=jnp.float32)  13.4 us
    unnamed x4, starting transfers between devices  13.2 us
  transfers between devices with their start and end apart: 7, of which 4 were waited for; matrix products, arithmetic and copies ran while one was open for 3% of the time, Pallas kernels for 0%

commit v1 on v0

v1 whole, which is shorter than its diff:
```python
import jax
import jax.numpy as jnp
from jax import lax
from jax.experimental import pallas as pl
from jax.experimental.pallas import tpu as pltpu
from jax.sharding import PartitionSpec as P

KIN = 128
KOUT = 128
TOK_SEQ = 64
N = 16
PAD = 16


def tail_kernel(
    left_ref, cot_ref, pout_ref, fisher_ref, stored_ref, out_ref,
    right_part, right_recv, right_own, right_all, left_recv,
    grads_own, grads_all, part, part_recv, prec_all, part2, part2_recv,
    send_sem, recv_sem, local_sem,
):
    row = lax.axis_index("row")
    col = lax.axis_index("col")
    tokens = cot_ref.shape[0]
    tok_blk = tokens // N
    seqs = tokens // TOK_SEQ

    def row_dev(d):
        return {"row": lax.rem(row + d, N), "col": col}

    def col_dev(d):
        return {"row": row, "col": lax.rem(col + d, N)}

    barrier = pltpu.get_barrier_semaphore()

    def greet(d, carry):
        pl.semaphore_signal(barrier, inc=1, device_id=row_dev(d))
        pl.semaphore_signal(barrier, inc=1, device_id=col_dev(d))
        return carry

    lax.fori_loop(1, N, greet, 0)

    right_part[...] = jnp.dot(cot_ref[...], pout_ref[...], preferred_element_type=jnp.float32)
    pl.semaphore_wait(barrier, 2 * (N - 1))

    def exchange(phase, src_of, dst_of, dev_of):
        def copy(d):
            return pltpu.make_async_remote_copy(
                src_ref=src_of(d), dst_ref=dst_of(d),
                send_sem=send_sem.at[phase, d], recv_sem=recv_sem.at[phase, d],
                device_id=dev_of(d),
            )

        def start(d, carry):
            copy(d).start()
            return carry

        def wait_recv(d, carry):
            copy(d).wait_recv()
            return carry

        def wait_send(d, carry):
            copy(d).wait_send()
            return carry

        lax.fori_loop(1, N, start, 0)
        return (
            lambda: lax.fori_loop(1, N, wait_recv, 0),
            lambda: lax.fori_loop(1, N, wait_send, 0),
        )

    def at_row(d):
        return lax.rem(row + d, N)

    def at_col(d):
        return lax.rem(col + d, N)

    right_in, right_sent = exchange(
        0, lambda d: right_part.at[pl.ds(at_row(d) * tok_blk, tok_blk)],
        lambda d: right_recv.at[d], row_dev)
    left_in, left_sent = exchange(
        1, lambda d: left_ref.at[pl.ds(at_row(d) * 8, 8)],
        lambda d: left_recv.at[d], row_dev)

    right_in()
    total = right_part[pl.ds(row * tok_blk, tok_blk), :]
    for d in range(1, N):
        total = total + right_recv[d]
    right_own[...] = total
    right_all[pl.ds(row * tok_blk, tok_blk), :] = total
    rall_in, rall_sent = exchange(
        2, lambda d: right_own,
        lambda d: right_all.at[pl.ds(row * tok_blk, tok_blk)], row_dev)

    left_in()
    left = left_ref[pl.ds(row * 8, 8), :]
    for d in range(1, N):
        left = left + left_recv[d]
    lane = lax.broadcasted_iota(jnp.int32, (PAD, tokens), 1)
    first = lax.broadcasted_iota(jnp.int32, (PAD, tokens), 0) * TOK_SEQ
    inside = (lane >= first) & (lane < first + TOK_SEQ)
    spread = jnp.concatenate(
        [jnp.where(inside, jnp.broadcast_to(left[i : i + 1, :], (PAD, tokens)), 0.0) for i in range(8)], axis=0)
    rall_in()
    grads = jnp.dot(spread, right_all[...], preferred_element_type=jnp.float32, precision=lax.Precision.HIGHEST)
    for i in range(8):
        piece = grads[i * PAD : (i + 1) * PAD, :].astype(jnp.bfloat16)
        grads_own[:, i * KOUT : (i + 1) * KOUT] = piece
        grads_all[pl.ds(pl.multiple_of(col * PAD, PAD), PAD), i * KOUT : (i + 1) * KOUT] = piece

    gall_in, gall_sent = exchange(
        3, lambda d: grads_own,
        lambda d: grads_all.at[pl.ds(col * PAD, PAD)], col_dev)
    gall_in()
    part[...] = jnp.dot(grads_all[...], fisher_ref[...], preferred_element_type=jnp.float32)
    part_in, part_sent = exchange(
        4, lambda d: part.at[pl.ds(at_row(d) * PAD, PAD)],
        lambda d: part_recv.at[d], row_dev)
    part_in()
    total = part[pl.ds(pl.multiple_of(row * PAD, PAD), PAD), :]
    for d in range(1, N):
        total = total + part_recv[d]
    own = total.astype(jnp.bfloat16)
    gall_sent()
    grads_own[...] = own
    prec_all[pl.ds(pl.multiple_of(row * PAD, PAD), PAD), :] = own
    pall_in, pall_sent = exchange(
        5, lambda d: grads_own,
        lambda d: prec_all.at[pl.ds(row * PAD, PAD)], row_dev)
    pall_in()
    part2[...] = lax.dot_general(
        prec_all[...], stored_ref[...], (((1,), (1,)), ((), ())), preferred_element_type=jnp.float32)
    part2_in, part2_sent = exchange(
        6, lambda d: part2.at[pl.ds(at_col(d) * PAD, PAD)],
        lambda d: part2_recv.at[d], col_dev)
    part2_in()
    total = part2[pl.ds(pl.multiple_of(col * PAD, PAD), PAD), :]
    for d in range(1, N):
        total = total + part2_recv[d]
    out_ref[...] = total[:seqs, :]
    for sent in (right_sent, left_sent, rall_sent, part_sent, pall_sent, part2_sent):
        sent()


def tail(left_t, cotangent, proj_out, fisher, stored):
    tokens = cotangent.shape[0]
    feats = fisher.shape[0]
    rows = N * PAD
    f32, bf16 = jnp.float32, jnp.bfloat16
    return pl.pallas_call(
        tail_kernel,
        out_shape=jax.ShapeDtypeStruct((tokens // TOK_SEQ, stored.shape[0]), f32),
        in_specs=[pl.BlockSpec(memory_space=pltpu.VMEM)] * 5,
        out_specs=pl.BlockSpec(memory_space=pltpu.VMEM),
        scratch_shapes=[
            pltpu.VMEM((tokens, KOUT), f32),
            pltpu.VMEM((N, tokens // N, KOUT), f32),
            pltpu.VMEM((tokens // N, KOUT), f32),
            pltpu.VMEM((tokens, KOUT), f32),
            pltpu.VMEM((N, 8, tokens), f32),
            pltpu.VMEM((PAD, feats), bf16),
            pltpu.VMEM((rows, feats), bf16),
            pltpu.VMEM((rows, feats), f32),
            pltpu.VMEM((N, PAD, feats), f32),
            pltpu.VMEM((rows, feats), bf16),
            pltpu.VMEM((rows, feats), f32),
            pltpu.VMEM((N, PAD, feats), f32),
            pltpu.SemaphoreType.DMA((7, N)),
            pltpu.SemaphoreType.DMA((7, N)),
            pltpu.SemaphoreType.DMA,
        ],
        compiler_params=pltpu.CompilerParams(
            collective_id=1, has_side_effects=True, vmem_limit_bytes=48 * 1024 * 1024),
        name="tail",
    )(left_t, cotangent, proj_out, fisher, stored)


def body(inputs, cotangent, gate_weight, up_weight, proj_in, proj_out, inverse_fisher, stored):
    gate_part = jnp.dot(
        inputs,
        lax.all_gather(gate_weight, "col", axis=0, tiled=True),
        preferred_element_type=jnp.float32,
    )
    up_part = jnp.dot(
        inputs,
        lax.all_gather(up_weight, "col", axis=0, tiled=True),
        preferred_element_type=jnp.float32,
    )
    hidden = (jax.nn.silu(gate_part) * up_part).astype(jnp.bfloat16)
    left_t = lax.dot_general(
        proj_in, hidden, (((0,), (1,)), ((), ())), preferred_element_type=jnp.float32)
    return tail(left_t, cotangent, proj_out, inverse_fisher, stored)


def solution(mesh):
    return jax.shard_map(
        body,
        mesh=mesh,
        in_specs=(
            P("col", None),
            P("col", "row"),
            P("col", "row"),
            P("col", "row"),
            P("row", None),
            P("row", None),
            P("row", "col"),
            P("row", "col"),
        ),
        out_specs=P("col", "row"),
        check_vma=False,
    )
```

time: 550 us -> 340 us (0.62)
  the two profiles are of different devices: /device:TPU:24 before, /device:TPU:7 now
where the time goes in v1:
time: 340 us
  waiting for transfers between devices  199 us (59%)
  Pallas kernels  101 us (30%)
  matrix products  24.6 us (7%)
  between operations  13.5 us (4%)
    all_gather x1, waiting for transfers between devices, body(): lax.all_gather(gate_weight, 'col', axis=0, tiled=True)  101 us
    pallas_call x1, Pallas kernels, tail(): pl.pallas_call(tail_kernel, out_shape=jax.ShapeDtypeStruct((tokens // TOK...  101 us
    all_gather x1, waiting for transfers between devices, body(): lax.all_gather(up_weight, 'col', axis=0, tiled=True)  96.4 us
    dot_general x1, matrix products, body(): lax.dot_general(proj_in, hidden, (((0,), (1,)), ((), ())), preferred_elem...  12.6 us
    dot_general x1, matrix products, body(): jnp.dot(inputs, lax.all_gather(gate_weight, 'col', axis=0, tiled=True), p...  11.9 us
  transfers between devices with their start and end apart: 2, of which 2 were waited for; matrix products, arithmetic and copies ran while one was open for 4% of the time, Pallas kernels for 0%

profile of v1, /device:TPU:7, one launch (start us, length us, event | category | flops | bytes accessed | tf_op | source)
XLA Modules:
  0.0 340.1 jit_solution(5971258376845899584)
XLA Ops:
  6.5 0.0 copy-start
  6.5 0.0 all-gather.3.cloned.1.call-start
  6.5 0.7 all-gather.3.cloned.1.call-update
  7.3 0.0 all-gather.5.cloned.1.call-start
  7.3 0.7 all-gather.5.cloned.1.call-update
  8.0 101.1 %all-gather.3.cloned.1.call-done = bf16[4096,896]{1,0:T(8,128)(2,1)} async-done(((bf16[256,896]{1,0:T(8,128)(2,1)}), bf16[4096,896]{1,0:T(8,128)(2,1)}) %all-gather.3.cloned.1.call-update) | async-done | bytes 7340048 | tf_op jit(solution)/shard_map/all_gather | solution.py:180
  109.1 11.9 %fusion.1 = f32[768,896]{1,0:T(8,128)} fusion(bf16[768,4096]{1,0:T(8,128)(2,1)} %param.8, bf16[4096,896]{1,0:T(8,128)(2,1)} %all-gather.3.cloned.1.call-done), kind=kOutput, calls=%fused_computation.3 | convolution fusion | flops 5637144576 | bytes 16384000 | tf_op jit(solution)/shard_map/dot_general | solution.py:178
  121.0 0.0 copy-start.1
  121.0 0.0 copy-start.3
  121.0 0.0 copy-start.4
  121.0 96.4 %all-gather.5.cloned.1.call-done = bf16[4096,896]{1,0:T(8,128)(2,1)} async-done(((bf16[256,896]{1,0:T(8,128)(2,1)}), bf16[4096,896]{1,0:T(8,128)(2,1)}) %all-gather.5.cloned.1.call-update) | async-done | bytes 7340048 | tf_op jit(solution)/shard_map/all_gather | solution.py:185
  217.5 0.0 copy-done
  217.5 12.6 %convolution_bitcast_fusion.left_ref = f32[128,768]{1,0:T(8,128)S(1)} fusion(bf16[896,128]{1,0:T(8,128)(2,1)S(1)} %copy-done, f32[768,896]{1,0:T(8,128)} %fusion.1, bf16[768,4096]{1,0:T(8,128)(2,1)} %param.8, bf16[4096,896]{1,0:T(8,128)(2,1)} %all-gather.5.cloned.1.call-done), kind=kOutput, calls=%fused_computation.1 | convolution fusion | flops 5817434112 | bytes 17006592 | tf_op jit(solution)/shard_map/dot_general | solution.py:189
  230.1 0.0 copy-done.1
  230.1 0.0 copy-done.3
  230.1 0.0 copy-done.4
  230.1 0.0 copy-start.2
  230.1 1.6 copy-done.2
  231.7 100.9 %tail.1 = f32[12,1024]{1,0:T(8,128)S(1)} custom-call(f32[128,768]{1,0:T(8,128)S(1)} %convolution_bitcast_fusion.left_ref, bf16[768,256]{1,0:T(8,128)(2,1)S(1)} %copy-done.3, bf16[256,128]{1,0:T(8,128)(2,1)S(1)} %copy-done.4, bf16[1024,1024]{1,0:T(8,128)(2,1)S(1)} %copy-done.1, bf16[1024,1024]{1,0:T(8,128)(2,1)S(1)} %copy-done.2), custom_call_target="tpu_custom_call" | custom-call | tf_op jit(solution)/shard_map/tail/pallas_call | solution.py:149
  332.6 0.6 copy.12
Async XLA Ops:
  6.5 210.9 %copy-start = (bf16[896,128]{1,0:T(8,128)(2,1)S(1)}, bf16[896,128]{1,0:T(8,128)(2,1)}, u32[]{:S(2)}) copy-start(bf16[896,128]{1,0:T(8,128)(2,1)} %param.12) | copy-start | bytes 688132
  6.5 102.6 %all-gather.3.cloned.1.call-start = ((), (), s32[]{:S(2)}) async-start(), calls=%async_computation | async-start | bytes 7798784 | tf_op jit(solution)/shard_map/all_gather | solution.py:180
  7.3 210.2 %all-gather.5.cloned.1.call-start = ((), (), s32[]{:S(2)}) async-start(), calls=%async_computation.1 | async-start | bytes 7798784 | tf_op jit(solution)/shard_map/all_gather | solution.py:185
  121.0 109.1 %copy-start.1 = (bf16[1024,1024]{1,0:T(8,128)(2,1)S(1)}, bf16[1024,1024]{1,0:T(8,128)(2,1)}, u32[]{:S(2)}) copy-start(bf16[1024,1024]{1,0:T(8,128)(2,1)} %fisher_ref.1) | copy-start | bytes 6291460
  121.0 109.1 %copy-start.3 = (bf16[768,256]{1,0:T(8,128)(2,1)S(1)}, bf16[768,256]{1,0:T(8,128)(2,1)}, u32[]{:S(2)}) copy-start(bf16[768,256]{1,0:T(8,128)(2,1)} %cot_ref.1) | copy-start | bytes 1179652
  121.0 109.1 %copy-start.4 = (bf16[256,128]{1,0:T(8,128)(2,1)S(1)}, bf16[256,128]{1,0:T(8,128)(2,1)}, u32[]{:S(2)}) copy-start(bf16[256,128]{1,0:T(8,128)(2,1)} %pout_ref.1) | copy-start | bytes 196612
  230.1 1.6 copy-start.2
Sparse Core Ops, SparseCore 0:
  9.8 99.2 all-gather.2
  111.5 105.8 all-gather.4

commit v2 on v1

--- a/solution.py
+++ b/solution.py
@@ -10,6 +10,319 @@
 TOK_SEQ = 64
 N = 16
 PAD = 16
+
+
+def place(zl, y, core, zh, x):
+    return {"row": (zl * 4 + y) * 2 + core, "col": zh * 4 + x}
+
+
+def ffn_kernel(
+    x_hbm, gate_hbm, up_hbm, pin_hbm, left_ref,
+    weights, acts, acc_gate, acc_up, pin,
+    local_sem, z_send, z_recv, x_send, x_recv, sib_send, sib_recv, in_send, in_recv,
+):
+    row = lax.axis_index("row")
+    col = lax.axis_index("col")
+    core = lax.rem(row, 2)
+    y = lax.rem(row // 2, 4)
+    zl = row // 8
+    x = lax.rem(col, 4)
+    zh = col // 4
+    kind = zh // 2
+    native = core == kind
+    beside = zh + 1 - 2 * lax.rem(zh, 2)
+    across = 3 - zh
+    across_beside = across + 1 - 2 * lax.rem(across, 2)
+    next_to_across = lax.rem(zh, 2) == zl
+    sources = (zh, beside, across, across_beside)
+    right = lax.rem(x + 1, 4)
+    left = lax.rem(x + 3, 4)
+    far = lax.rem(x + 2, 4)
+    up_y = lax.rem(y + 1, 4)
+    down_y = lax.rem(y + 3, 4)
+    far_y = lax.rem(y + 2, 4)
+    depth = gate_hbm.shape[0]
+    group = 4 * depth
+    tokens = x_hbm.shape[0]
+    quarter = tokens // 4
+    sibling = place(zl, y, 1 - core, zh, x)
+
+    barrier = pltpu.get_barrier_semaphore()
+    partners = [
+        sibling,
+        place(zl, y, 0, beside, x), place(zl, y, 1, beside, x),
+        place(zl, y, 0, across, x), place(zl, y, 1, across, x),
+        place(zl, y, core, zh, right), place(zl, y, core, zh, left),
+        place(zl, up_y, core, zh, x), place(zl, down_y, core, zh, x),
+        place(1 - zl, y, core, zh, x), place(1 - zl, y, core, across, x),
+    ]
+    for partner in partners:
+        pl.semaphore_signal(barrier, inc=1, device_id=partner)
+    pl.semaphore_wait(barrier, len(partners))
+
+    def remote(src, dst, send, recv, device):
+        return pltpu.make_async_remote_copy(
+            src_ref=src, dst_ref=dst, send_sem=send, recv_sem=recv, device_id=device)
+
+    def block(m, zs, xs, start=0, rows=depth):
+        return weights.at[m, pl.ds(zs * group + xs * depth + start, rows)]
+
+    mats = (gate_hbm, up_hbm)
+
+    def start_z(m, device, j, slot):
+        return remote(mats[m], block(m, zh, x), z_send.at[slot], z_recv.at[j], device)
+
+    def z_arrival(j):
+        return remote(block(core, sources[j], x), block(core, sources[j], x),
+                      z_send.at[3], z_recv.at[j], sibling)
+
+    def in_copy(src_ref, q, start, rows, slot_send, slot_recv, device):
+        at = pl.ds(q * quarter + start, rows)
+        return remote(src_ref.at[at], acts.at[at], in_send.at[slot_send], in_recv.at[slot_recv], device)
+
+    acts_copy = pltpu.make_async_copy(x_hbm, acts, local_sem.at[0])
+    pin_copy = pltpu.make_async_copy(pin_hbm, pin, local_sem.at[1])
+    pin_remote = remote(pin_hbm, pin, in_send.at[0], in_recv.at[0], sibling)
+    quarter_out = in_copy(x_hbm, y, 0, quarter, 1, 1, place(1 - zl, y, core, across, x))
+    quarter_on = in_copy(acts, y, 0, quarter, 2, 1, place(1 - zl, y, core, zh, x))
+    quarter_up = in_copy(acts, y, 0, quarter, 3, 2, place(zl, up_y, core, zh, x))
+    quarter_down = in_copy(acts, y, 0, quarter, 4, 3, place(zl, down_y, core, zh, x))
+    half_up = in_copy(acts, down_y, 0, quarter // 2, 5, 4, place(zl, up_y, core, zh, x))
+    half_down = in_copy(acts, up_y, quarter // 2, quarter // 2, 6, 5, place(zl, down_y, core, zh, x))
+
+    for m in range(2):
+        own_copy = pltpu.make_async_copy(mats[m], block(m, zh, x), local_sem.at[2])
+
+        @pl.when(native & (core == m))
+        def _():
+            own_copy.start()
+
+    @pl.when(native)
+    def _():
+        for m in range(2):
+
+            @pl.when(core != m)
+            def _():
+                start_z(m, sibling, 0, 2).start()
+
+        for m in range(2):
+            start_z(m, place(zl, y, m, beside, x), 1, m).start()
+        for m in range(2):
+
+            @pl.when(core == m)
+            def _():
+                pltpu.make_async_copy(mats[m], block(m, zh, x), local_sem.at[2]).wait()
+
+        pin_remote.start()
+        pin_copy.start()
+        acts_copy.start()
+
+        @pl.when(next_to_across)
+        def _():
+            quarter_out.start()
+
+    @pl.when(jnp.logical_not(native))
+    def _():
+        for m in range(2):
+            start_z(m, place(zl, y, m, across, x), 2, m).start()
+        z_arrival(0).wait_recv()
+
+    def sib_copy(j, k):
+        xs = (x, left, right, far)[k]
+        return remote(block(core, sources[j], xs), block(core, sources[j], xs),
+                      sib_send.at[j, k], sib_recv.at[j, k], sibling)
+
+    def x_copy(j, k):
+        zs = sources[j]
+        half = depth // 2
+        ref, device = {
+            0: (block(core, zs, x), right),
+            1: (block(core, zs, x), left),
+            2: (block(core, zs, left, 0, half), right),
+            3: (block(core, zs, right, half, half), left),
+        }[k]
+        return remote(ref, ref, x_send.at[j, k], x_recv.at[j, k], place(zl, y, core, zh, device))
+
+    z_forward = remote(block(core, across, x), block(core, across, x),
+                       z_send.at[3], z_recv.at[3], place(zl, y, core, beside, x))
+
+    def have_column(j):
+        if j > 0:
+            z_arrival(j).wait_recv()
+        if j == 2:
+            z_forward.start()
+        x_copy(j, 0).start()
+        x_copy(j, 1).start()
+        sib_copy(j, 0).start()
+
+    def have_sides(j):
+        for k in range(2):
+            x_copy(j, k).wait_recv()
+            x_copy(j, 2 + k).start()
+            sib_copy(j, 1 + k).start()
+
+    def have_far(j):
+        x_copy(j, 2).wait_recv()
+        x_copy(j, 3).wait_recv()
+        sib_copy(j, 3).start()
+
+    def sib_arrival(j):
+        for k in range(4):
+            xs = (x, left, right, far)[k]
+            remote(block(1 - core, sources[j], xs), block(1 - core, sources[j], xs),
+                   sib_send.at[j, k], sib_recv.at[j, k], sibling).wait_recv()
+
+    def quarter_in():
+        return remote(acts.at[pl.ds(y * quarter, quarter)], acts.at[pl.ds(y * quarter, quarter)],
+                      in_send.at[1], in_recv.at[1], sibling)
+
+    have_column(0)
+    have_column(1)
+    have_sides(0)
+    have_column(2)
+
+    @pl.when(jnp.logical_not(native))
+    def _():
+        quarter_in().wait_recv()
+
+        @pl.when(next_to_across)
+        def _():
+            quarter_on.start()
+
+        quarter_up.start()
+        quarter_down.start()
+
+    have_far(0)
+    have_sides(1)
+    have_column(3)
+    have_far(1)
+    have_sides(2)
+
+    @pl.when(jnp.logical_not(native))
+    def _():
+        quarter_up.wait_recv()
+        half_up.start()
+        quarter_down.wait_recv()
+        half_down.start()
+
+    have_far(2)
+
+    @pl.when(jnp.logical_not(native))
+    def _():
+        half_up.wait_recv()
+        half_down.wait_recv()
+        pin_remote.wait_recv()
+
+    @pl.when(native)
+    def _():
+        acts_copy.wait()
+        pin_copy.wait()
+
+    tile = 256
+
+    def products(j, t):
+        rows = pl.ds(pl.multiple_of(t * tile, tile), tile)
+        deep = pl.ds(pl.multiple_of(sources[j] * group, group), group)
+        a = acts[rows, deep]
+        gate = jnp.dot(a, weights[0, deep, :], preferred_element_type=jnp.float32)
+        up = jnp.dot(a, weights[1, deep, :], preferred_element_type=jnp.float32)
+        return rows, gate, up
+
+    def compute(j):
+        sib_arrival(j)
+
+        def step(t, carry):
+            rows, gate, up = products(j, t)
+            if j == 0:
+                acc_gate[rows, :] = gate
+                acc_up[rows, :] = up
+            else:
+                acc_gate[rows, :] += gate
+                acc_up[rows, :] += up
+            return carry
+
+        lax.fori_loop(0, tokens // tile, step, 0)
+
+    compute(0)
+    have_sides(3)
+    compute(1)
+    compute(2)
+    have_far(3)
+    sib_arrival(3)
+
+    def finish(t, carry):
+        rows, gate, up = products(3, t)
+        gate = acc_gate[rows, :] + gate
+        up = acc_up[rows, :] + up
+        hidden = (gate / (1.0 + jnp.exp(-gate)) * up).astype(jnp.bfloat16)
+        left_ref[:, rows] = lax.dot_general(
+            pin[...], hidden, (((0,), (1,)), ((), ())), preferred_element_type=jnp.float32)
+        return carry
+
+    lax.fori_loop(0, tokens // tile, finish, 0)
+
+    @pl.when(native)
+    def _():
+        for m in range(2):
+            start_z(m, place(zl, y, m, beside, x), 1, m).wait_send()
+
+            @pl.when(core != m)
+            def _():
+                start_z(m, sibling, 0, 2).wait_send()
+
+        pin_remote.wait_send()
+
+        @pl.when(next_to_across)
+        def _():
+            quarter_out.wait_send()
+
+    @pl.when(jnp.logical_not(native))
+    def _():
+        for m in range(2):
+            start_z(m, place(zl, y, m, across, x), 2, m).wait_send()
+
+        @pl.when(next_to_across)
+        def _():
+            quarter_on.wait_send()
+
+        quarter_up.wait_send()
+        quarter_down.wait_send()
+        half_up.wait_send()
+        half_down.wait_send()
+
+    z_forward.wait_send()
+    for j in range(4):
+        for k in range(4):
+            x_copy(j, k).wait_send()
+            sib_copy(j, k).wait_send()
+
+
+def ffn(inputs, gate_weight, up_weight, proj_in):
+    tokens, width = inputs.shape
+    units = gate_weight.shape[1]
+    f32, bf16 = jnp.float32, jnp.bfloat16
+    dma = pltpu.SemaphoreType.DMA
+    return pl.pallas_call(
+        ffn_kernel,
+        out_shape=jax.ShapeDtypeStruct((KIN, tokens), f32),
+        in_specs=[pl.BlockSpec(memory_space=pl.ANY)] * 4,
+        out_specs=pl.BlockSpec(memory_space=pltpu.VMEM),
+        scratch_shapes=[
+            pltpu.VMEM((2, width, units), bf16),
+            pltpu.VMEM((tokens, width), bf16),
+            pltpu.VMEM((tokens, units), f32),
+            pltpu.VMEM((tokens, units), f32),
+            pltpu.VMEM((units, KIN), bf16),
+            dma((3,)),
+            dma((4,)), dma((4,)),
+            dma((4, 4)), dma((4, 4)),
+            dma((4, 4)), dma((4, 4)),
+            dma((7,)), dma((6,)),
+        ],
+        compiler_params=pltpu.CompilerParams(
+            collective_id=2, has_side_effects=True, vmem_limit_bytes=56 * 1024 * 1024),
+        name="ffn",
+    )(inputs, gate_weight, up_weight, proj_in)
 
 
 def tail_kernel(
@@ -30,17 +343,26 @@
     def col_dev(d):
         return {"row": row, "col": lax.rem(col + d, N)}
 
+    x = lax.rem(col, 4)
+    zh = col // 4
+    kind = zh // 2
+    core = lax.rem(row, 2)
+    native = core == kind
+    across = (3 - zh) * 4 + x
+    target = jnp.where(native, col, across)
+
     barrier = pltpu.get_barrier_semaphore()
 
     def greet(d, carry):
         pl.semaphore_signal(barrier, inc=1, device_id=row_dev(d))
         pl.semaphore_signal(barrier, inc=1, device_id=col_dev(d))
+        pl.semaphore_signal(barrier, inc=1, device_id={"row": lax.rem(row + d, N), "col": across})
         return carry
 
     lax.fori_loop(1, N, greet, 0)
 
     right_part[...] = jnp.dot(cot_ref[...], pout_ref[...], preferred_element_type=jnp.float32)
-    pl.semaphore_wait(barrier, 2 * (N - 1))
+    pl.semaphore_wait(barrier, 3 * (N - 1))
 
     def exchange(phase, src_of, dst_of, dev_of):
         def copy(d):
@@ -77,9 +399,55 @@
     right_in, right_sent = exchange(
         0, lambda d: right_part.at[pl.ds(at_row(d) * tok_blk, tok_blk)],
         lambda d: right_recv.at[d], row_dev)
-    left_in, left_sent = exchange(
-        1, lambda d: left_ref.at[pl.ds(at_row(d) * 8, 8)],
-        lambda d: left_recv.at[d], row_dev)
+    slot = row - core + jnp.where(native, 0, 1)
+
+    def left_copy(d):
+        to = at_row(d)
+        return pltpu.make_async_remote_copy(
+            src_ref=left_ref.at[pl.ds(to * 8, 8)], dst_ref=left_recv.at[slot],
+            send_sem=send_sem.at[1, d], recv_sem=recv_sem.at[1, slot],
+            device_id={"row": to, "col": target})
+
+    def left_start(d, carry):
+        left_copy(d).start()
+        return carry
+
+    lax.fori_loop(1, N, left_start, 0)
+
+    @pl.when(native)
+    def _():
+        own_left = pltpu.make_async_copy(
+            left_ref.at[pl.ds(row * 8, 8)], left_recv.at[slot], local_sem)
+        own_left.start()
+        own_left.wait()
+
+    @pl.when(jnp.logical_not(native))
+    def _():
+        left_copy(0).start()
+
+    def left_in():
+        def wait_one(s, carry):
+            @pl.when(jnp.logical_not(native & (s == slot)))
+            def _():
+                pltpu.make_async_remote_copy(
+                    src_ref=left_recv.at[s], dst_ref=left_recv.at[s],
+                    send_sem=send_sem.at[1, 0], recv_sem=recv_sem.at[1, s],
+                    device_id={"row": lax.rem(row + 1, N), "col": col}).wait_recv()
+
+            return carry
+
+        lax.fori_loop(0, N, wait_one, 0)
+
+    def left_sent():
+        def wait_one(d, carry):
+            left_copy(d).wait_send()
+            return carry
+
+        lax.fori_loop(1, N, wait_one, 0)
+
+        @pl.when(jnp.logical_not(native))
+        def _():
+            left_copy(0).wait_send()
 
     right_in()
     total = right_part[pl.ds(row * tok_blk, tok_blk), :]
@@ -92,7 +460,7 @@
         lambda d: right_all.at[pl.ds(row * tok_blk, tok_blk)], row_dev)
 
     left_in()
-    left = left_ref[pl.ds(row * 8, 8), :]
+    left = left_recv[0]
     for d in range(1, N):
         left = left + left_recv[d]
     lane = lax.broadcasted_iota(jnp.int32, (PAD, tokens), 1)
@@ -175,19 +543,7 @@
 
 
 def body(inputs, cotangent, gate_weight, up_weight, proj_in, proj_out, inverse_fisher, stored):
-    gate_part = jnp.dot(
-        inputs,
-        lax.all_gather(gate_weight, "col", axis=0, tiled=True),
-        preferred_element_type=jnp.float32,
-    )
-    up_part = jnp.dot(
-        inputs,
-        lax.all_gather(up_weight, "col", axis=0, tiled=True),
-        preferred_element_type=jnp.float32,
-    )
-    hidden = (jax.nn.silu(gate_part) * up_part).astype(jnp.bfloat16)
-    left_t = lax.dot_general(
-        proj_in, hidden, (((0,), (1,)), ((), ())), preferred_element_type=jnp.float32)
+    left_t = ffn(inputs, gate_weight, up_weight, proj_in)
     return tail(left_t, cotangent, proj_out, inverse_fisher, stored)
 
 

time: 340 us -> 210 us (0.62)
  the two profiles are of different devices: /device:TPU:7 before, /device:TPU:24 now
where the time goes in v2:
time: 210 us; the launch traced here: 208 us
  Pallas kernels  206 us (98%)
    pallas_call x1, Pallas kernels, tail(): pl.pallas_call(tail_kernel, out_shape=jax.ShapeDtypeStruct((tokens // TOK...  110 us
    pallas_call x1, Pallas kernels, ffn(): pl.pallas_call(ffn_kernel, out_shape=jax.ShapeDtypeStruct((KIN, tokens),...  95.9 us

profile of v2, /device:TPU:24, one launch (start us, length us, event | category | flops | bytes accessed | tf_op | source)
XLA Modules:
  0.0 208.1 jit_solution(14356254001304106677)
XLA Ops:
  0.0 0.0 copy-start.1
  0.0 0.0 copy-start
  0.0 0.0 copy-start.4
  0.0 0.0 copy-start.3
  0.0 95.9 %ffn.1.left_ref = f32[128,768]{1,0:T(8,128)} custom-call(bf16[768,4096]{1,0:T(8,128)(2,1)} %x_hbm.1, bf16[256,896]{1,0:T(8,128)(2,1)} %gate_hbm.1, bf16[256,896]{1,0:T(8,128)(2,1)} %up_hbm.1, bf16[896,128]{1,0:T(8,128)(2,1)} %pin_hbm.1), custom_call_target="tpu_custom_call" | custom-call | tf_op jit(solution)/shard_map/ffn/pallas_call | solution.py:305
  95.9 0.0 copy-done.1
  95.9 0.0 copy-done
  95.9 0.0 copy-done.4
  95.9 0.0 copy-done.3
  95.9 0.0 copy-start.2
  96.0 1.0 copy-done.2
  96.9 110.5 %tail.1 = f32[12,1024]{1,0:T(8,128)S(1)} custom-call(f32[128,768]{1,0:T(8,128)S(1)} %copy-done.2, bf16[768,256]{1,0:T(8,128)(2,1)S(1)} %copy-done.3, bf16[256,128]{1,0:T(8,128)(2,1)S(1)} %copy-done.4, bf16[1024,1024]{1,0:T(8,128)(2,1)S(1)} %copy-done, bf16[1024,1024]{1,0:T(8,128)(2,1)S(1)} %copy-done.1), custom_call_target="tpu_custom_call" | custom-call | tf_op jit(solution)/shard_map/tail/pallas_call | solution.py:517
  207.4 0.6 copy.10
Async XLA Ops:
  0.0 95.9 %copy-start.1 = (bf16[1024,1024]{1,0:T(8,128)(2,1)S(1)}, bf16[1024,1024]{1,0:T(8,128)(2,1)}, u32[]{:S(2)}) copy-start(bf16[1024,1024]{1,0:T(8,128)(2,1)} %stored_ref.1) | copy-start | bytes 6291460
  0.0 95.9 %copy-start = (bf16[1024,1024]{1,0:T(8,128)(2,1)S(1)}, bf16[1024,1024]{1,0:T(8,128)(2,1)}, u32[]{:S(2)}) copy-start(bf16[1024,1024]{1,0:T(8,128)(2,1)} %fisher_ref.1) | copy-start | bytes 6291460
  0.0 95.9 %copy-start.4 = (bf16[256,128]{1,0:T(8,128)(2,1)S(1)}, bf16[256,128]{1,0:T(8,128)(2,1)}, u32[]{:S(2)}) copy-start(bf16[256,128]{1,0:T(8,128)(2,1)} %pout_ref.1) | copy-start | bytes 196612
  0.0 95.9 %copy-start.3 = (bf16[768,256]{1,0:T(8,128)(2,1)S(1)}, bf16[768,256]{1,0:T(8,128)(2,1)}, u32[]{:S(2)}) copy-start(bf16[768,256]{1,0:T(8,128)(2,1)} %cot_ref.1) | copy-start | bytes 1179652
  95.9 1.0 copy-start.2

commit v3 on v0

v3 whole, which is shorter than its diff:
```python
import jax
import jax.numpy as jnp
from jax import lax
from jax.experimental import pallas as pl
from jax.experimental.pallas import tpu as pltpu
from jax.sharding import PartitionSpec as P

KIN = 128
KOUT = 128
TOK_SEQ = 64
N = 16
PAD = 16
TILE = 256


def place(zl, y, core, zh, x):
    return {"row": (zl * 4 + y) * 2 + core, "col": zh * 4 + x}


def remote(src, dst, send, recv, device):
    return pltpu.make_async_remote_copy(
        src_ref=src, dst_ref=dst, send_sem=send, recv_sem=recv, device_id=device)


def scores_kernel(
    x_hbm, cot_hbm, gate_hbm, up_hbm, pin_hbm, pout_hbm, fisher_hbm, stored_hbm, out_ref,
    weights, acts, acc_gate, acc_up, pin, cot, pout, fisher, stored,
    left_part, left_recv, right_part, right_recv, right_own, right_all,
    grads_all, part, part_recv, prec_own, prec_all, part2, part2_recv, fold, fold_recv,
    local_sem, z_send, z_recv, x_send, x_recv, sib_send, sib_recv, in_send, in_recv,
    tail_send, tail_recv,
):
    row = lax.axis_index("row")
    col = lax.axis_index("col")
    core = lax.rem(row, 2)
    y = lax.rem(row // 2, 4)
    zl = row // 8
    x = lax.rem(col, 4)
    zh = col // 4
    kind = zh // 2
    native = core == kind
    foreign = core != kind
    beside = zh + 1 - 2 * lax.rem(zh, 2)
    across = 3 - zh
    across_beside = across + 1 - 2 * lax.rem(across, 2)
    next_to_across = lax.rem(zh, 2) == zl
    sources = (zh, beside, across, across_beside)
    right = lax.rem(x + 1, 4)
    left = lax.rem(x + 3, 4)
    far = lax.rem(x + 2, 4)
    sides = (x, left, right, far)
    up_y = lax.rem(y + 1, 4)
    down_y = lax.rem(y + 3, 4)
    depth = gate_hbm.shape[0]
    sub = depth // 2
    group = 4 * depth
    tokens = x_hbm.shape[0]
    quarter = tokens // 4
    eighth = quarter // 2
    tok_blk = tokens // N
    seqs = tokens // TOK_SEQ
    sibling = place(zl, y, 1 - core, zh, x)
    token_col = jnp.where(native, zh, across) * 4 + x

    def row_dev(d):
        return {"row": lax.rem(row + d, N), "col": col}

    loads = [
        pltpu.make_async_copy(a, b, local_sem.at[i])
        for i, (a, b) in enumerate(
            [(cot_hbm, cot), (pout_hbm, pout), (fisher_hbm, fisher), (stored_hbm, stored)])
    ]
    acts_copy = pltpu.make_async_copy(x_hbm, acts, local_sem.at[4])
    pin_copy = pltpu.make_async_copy(pin_hbm, pin, local_sem.at[5])
    for load in loads:
        load.start()

    barrier = pltpu.get_barrier_semaphore()
    partners = [row_dev(d) for d in range(1, N)]
    partners += [{"row": lax.rem(row + d, N), "col": across * 4 + x} for d in range(N)]
    partners += [place(zl, y, 0, beside, x), place(zl, y, 1, beside, x), place(zl, y, core, across_beside, x)]
    partners += [place(zl, y, core, zh, side) for side in (right, left, far)]
    for partner in partners:
        pl.semaphore_signal(barrier, inc=1, device_id=partner)
    pl.semaphore_wait(barrier, len(partners))

    def block(m, zs, xs, start=0, rows=depth):
        return weights.at[m, pl.ds(zs * group + xs * depth + start, rows)]

    mats = (gate_hbm, up_hbm)

    def z_copy(m, s, device, j, slot):
        return remote(mats[m].at[pl.ds(s * sub, sub)], block(m, zh, x, s * sub, sub),
                      z_send.at[slot, s], z_recv.at[j, s], device)

    def z_forward(s):
        ref = block(core, across, x, s * sub, sub)
        return remote(ref, ref, z_send.at[3, s], z_recv.at[3, s], place(zl, y, core, beside, x))

    def z_arrival(j, s):
        ref = block(core, sources[j], x, s * sub, sub)
        return remote(ref, ref, z_send.at[3, s], z_recv.at[j, s], sibling)

    def in_copy(src_ref, q, s, slot, recv_slot, device):
        at = pl.ds(q * quarter + s * eighth, eighth)
        return remote(src_ref.at[at], acts.at[at], in_send.at[slot], in_recv.at[recv_slot], device)

    pin_remote = remote(pin_hbm, pin, in_send.at[0], in_recv.at[0], sibling)

    def quarter_out(s):
        return in_copy(x_hbm, y, s, 1 + s, 1 + s, place(1 - zl, y, core, across, x))

    def quarter_on(s):
        return in_copy(acts, y, s, 3 + s, 1 + s, place(1 - zl, y, core, zh, x))

    def quarter_up(s):
        return in_copy(acts, y, s, 5 + s, 5 + s, place(zl, up_y, core, zh, x))

    def quarter_down(s):
        return in_copy(acts, y, s, 7 + s, 7 + s, place(zl, down_y, core, zh, x))

    half_up = in_copy(acts, down_y, 0, 9, 9, place(zl, up_y, core, zh, x))
    half_down = in_copy(acts, up_y, 1, 10, 10, place(zl, down_y, core, zh, x))

    def own_copy(m):
        return pltpu.make_async_copy(mats[m], block(m, zh, x), local_sem.at[6])

    @pl.when(native)
    def _():
        for m in range(2):

            @pl.when(core == m)
            def _():
                own_copy(m).start()

            @pl.when(core != m)
            def _():
                for s in range(2):
                    z_copy(m, s, sibling, 0, 2).start()

        @pl.when(next_to_across)
        def _():
            for s in range(2):
                quarter_out(s).start()

        for s in range(2):
            for m in range(2):
                z_copy(m, s, place(zl, y, m, beside, x), 1, m).start()
        for m in range(2):

            @pl.when(core == m)
            def _():
                own_copy(m).wait()

        pin_remote.start()
        pin_copy.start()
        acts_copy.start()

    def across_start(s):
        @pl.when(foreign)
        def _():
            for m in range(2):
                z_copy(m, s, place(zl, y, m, across, x), 2, m).start()

    def sib_copy(j, k):
        ref = block(core, sources[j], sides[k])
        return remote(ref, ref, sib_send.at[j, k], sib_recv.at[j, k], sibling)

    def x_copy(j, k):
        side, s = (k // 2, k % 2) if k < 4 else (k - 4, k - 4)
        whose = x if k < 4 else (left, right)[side]
        ref = block(core, sources[j], whose, s * sub, sub)
        return remote(ref, ref, x_send.at[j, k], x_recv.at[j, k],
                      place(zl, y, core, zh, (right, left)[side]))

    def have_column(j, s):
        if j > 0:
            z_arrival(j, s).wait_recv()
        else:

            @pl.when(foreign)
            def _():
                z_arrival(0, s).wait_recv()

        if j == 2:
            z_forward(s).start()
        x_copy(j, s).start()
        x_copy(j, 2 + s).start()
        if s == 1:
            sib_copy(j, 0).start()

    def have_side(j, s):
        for side in range(2):
            x_copy(j, 2 * side + s).wait_recv()
            if s == side:
                x_copy(j, 4 + s).start()
            if s == 1:
                sib_copy(j, 1 + side).start()

    def have_far(j):
        x_copy(j, 4).wait_recv()
        x_copy(j, 5).wait_recv()
        sib_copy(j, 3).start()

    def sib_arrival(j, k):
        ref = block(1 - core, sources[j], sides[k])
        remote(ref, ref, sib_send.at[j, k], sib_recv.at[j, k], sibling).wait_recv()

    def have_quarter(s):
        @pl.when(foreign)
        def _():
            quarter_out(s).wait_recv()

            @pl.when(next_to_across)
            def _():
                quarter_on(s).start()

            quarter_up(s).start()
            quarter_down(s).start()

    def pass_quarters():
        @pl.when(foreign)
        def _():
            quarter_up(0).wait_recv()
            half_up.start()
            quarter_up(1).wait_recv()
            quarter_down(0).wait_recv()
            quarter_down(1).wait_recv()
            half_down.start()

    def have_inputs():
        @pl.when(foreign)
        def _():
            half_up.wait_recv()
            half_down.wait_recv()
            pin_remote.wait_recv()

        @pl.when(native)
        def _():
            acts_copy.wait()
            pin_copy.wait()

    def many(phase, src_of, dst_of, dev_of, first=1, last=N):
        def copy(d):
            return remote(src_of(d), dst_of(d), tail_send.at[phase, d], tail_recv.at[phase, d], dev_of(d))

        def run(action):
            def step(d, carry):
                action(copy(d))
                return carry

            lax.fori_loop(first, last, step, 0)

        run(lambda c: c.start())
        return lambda: run(lambda c: c.wait_recv()), lambda: run(lambda c: c.wait_send())

    def at_row(d):
        return lax.rem(row + d, N)

    def deep_dot(j, rows, start=0, size=group):
        deep = pl.ds(pl.multiple_of(sources[j] * group + start, 256), size)
        a = acts[rows, deep]
        return (jnp.dot(a, weights[0, deep, :], preferred_element_type=jnp.float32),
                jnp.dot(a, weights[1, deep, :], preferred_element_type=jnp.float32))

    def tiles(step):
        def at(t, carry):
            step(pl.ds(pl.multiple_of(t * TILE, TILE), TILE))
            return carry

        lax.fori_loop(0, tokens // TILE, at, 0)

    def compute_first():
        def step(rows):
            gate, up = deep_dot(0, rows)
            acc_gate[rows, :] = gate
            acc_up[rows, :] = up

        tiles(step)

    def compute_add(j):
        def step(rows):
            gate, up = deep_dot(j, rows)
            acc_gate[rows, :] += gate
            acc_up[rows, :] += up

        tiles(step)

    def sibs(j):
        for k in range(4):
            sib_arrival(j, k)

    have_column(0, 0)
    have_column(0, 1)
    loads[0].wait()
    loads[1].wait()
    right_part[...] = jnp.dot(cot[...], pout[...], preferred_element_type=jnp.float32)
    right_in, right_sent = many(
        0, lambda d: right_part.at[pl.ds(at_row(d) * tok_blk, tok_blk)],
        lambda d: right_recv.at[d], row_dev)
    have_side(0, 0)
    across_start(0)
    have_quarter(0)
    have_column(1, 0)
    have_side(0, 1)
    across_start(1)
    have_quarter(1)
    have_column(1, 1)
    have_far(0)
    have_column(2, 0)
    have_side(1, 0)
    have_side(1, 1)
    have_column(2, 1)

    right_in()
    total = right_part[pl.ds(row * tok_blk, tok_blk), :]
    for d in range(1, N):
        total = total + right_recv[d]
    right_own[...] = total
    right_all[pl.ds(row * tok_blk, tok_blk), :] = total
    rall_in, rall_sent = many(
        2, lambda d: right_own,
        lambda d: right_all.at[pl.ds(row * tok_blk, tok_blk)], row_dev)

    have_column(3, 0)
    pass_quarters()
    have_far(1)
    have_side(2, 0)
    have_side(2, 1)
    have_column(3, 1)
    have_inputs()
    sibs(0)
    compute_first()
    have_far(2)
    have_side(3, 0)
    have_side(3, 1)
    sibs(1)
    compute_add(1)
    sibs(2)
    compute_add(2)
    have_far(3)
    sibs(3)

    def finish(rows):
        gate, up = deep_dot(3, rows)
        gate = acc_gate[rows, :] + gate
        up = acc_up[rows, :] + up
        hidden = (gate / (1.0 + jnp.exp(-gate)) * up).astype(jnp.bfloat16)
        left_part[:, rows] = lax.dot_general(
            pin[...], hidden, (((0,), (1,)), ((), ())), preferred_element_type=jnp.float32)

    tiles(finish)

    slot = row - core + jnp.where(native, 0, 1)

    def left_copy(d):
        to = at_row(d)
        return remote(left_part.at[pl.ds(to * 8, 8)], left_recv.at[slot],
                      tail_send.at[1, d], tail_recv.at[1, slot], {"row": to, "col": token_col})

    def left_start(d, carry):
        left_copy(d).start()
        return carry

    lax.fori_loop(1, N, left_start, 0)

    @pl.when(native)
    def _():
        left_recv[pl.ds(slot, 1)] = left_part[pl.ds(row * 8, 8), :][None]

    @pl.when(foreign)
    def _():
        left_copy(0).start()

    rall_in()

    def left_wait(s, carry):
        @pl.when(foreign | (s != slot))
        def _():
            remote(left_recv.at[s], left_recv.at[s], tail_send.at[1, 0], tail_recv.at[1, s], sibling).wait_recv()

        return carry

    lax.fori_loop(0, N, left_wait, 0)
    total = left_recv[0]
    for d in range(1, N):
        total = total + left_recv[d]
    lane = lax.broadcasted_iota(jnp.int32, (PAD, tokens), 1)
    first = lax.broadcasted_iota(jnp.int32, (PAD, tokens), 0) * TOK_SEQ
    inside = (lane >= first) & (lane < first + TOK_SEQ)
    spread = jnp.concatenate(
        [jnp.where(inside, jnp.broadcast_to(total[i : i + 1, :], (PAD, tokens)), 0.0) for i in range(8)], axis=0)
    grads = jnp.dot(spread, right_all[...], preferred_element_type=jnp.float32, precision=lax.Precision.HIGHEST)
    mine = pl.ds(pl.multiple_of((x * 4 + zh) * PAD, PAD), PAD)
    column = pl.ds(pl.multiple_of(x * 4 * PAD, PAD), 4 * PAD)
    for i in range(8):
        grads_all[mine, i * KOUT : (i + 1) * KOUT] = grads[i * PAD : (i + 1) * PAD, :].astype(jnp.bfloat16)

    def z_dev(d):
        return place(zl, y, core, lax.rem(zh + d, 4), x)

    def x_dev(d):
        return place(zl, y, core, zh, lax.rem(x + d, 4))

    gz_in, gz_sent = many(3, lambda d: grads_all.at[mine], lambda d: grads_all.at[mine], z_dev, 1, 4)
    gz_in()
    gx_in, gx_sent = many(
        3, lambda d: grads_all.at[column], lambda d: grads_all.at[column], lambda d: x_dev(d - 3), 4, 7)
    loads[2].wait()
    gx_in()
    part[...] = jnp.dot(
        grads_all[...], fisher[...], preferred_element_type=jnp.float32).astype(jnp.bfloat16)
    part_in, part_sent = many(
        4, lambda d: part.at[pl.ds(at_row(d) * PAD, PAD)],
        lambda d: part_recv.at[d], row_dev)
    row_rows = pl.ds(pl.multiple_of(row * PAD, PAD), PAD)
    part_in()
    total = part[row_rows, :].astype(jnp.float32)
    for d in range(1, N):
        total = total + part_recv[d].astype(jnp.float32)
    prec_own[...] = total.astype(jnp.bfloat16)
    prec_all[row_rows, :] = total.astype(jnp.bfloat16)
    pall_in, pall_sent = many(
        5, lambda d: prec_own, lambda d: prec_all.at[pl.ds(row * PAD, PAD)], row_dev)
    loads[3].wait()
    pall_in()
    part2[...] = lax.dot_general(
        prec_all[...], stored[...], (((1,), (1,)), ((), ())), preferred_element_type=jnp.float32).astype(jnp.bfloat16)
    sx_in, sx_sent = many(
        6, lambda d: part2.at[pl.ds(lax.rem(x + d, 4) * 4 * PAD, 4 * PAD)],
        lambda d: part2_recv.at[d], x_dev, 1, 4)
    sx_in()
    total = part2[column, :].astype(jnp.float32)
    for d in range(1, 4):
        total = total + part2_recv[d].astype(jnp.float32)
    fold[...] = total
    sz_in, sz_sent = many(
        6, lambda d: fold.at[pl.ds(lax.rem(zh + d - 3, 4) * PAD, PAD)],
        lambda d: fold_recv.at[d - 3], lambda d: z_dev(d - 3), 4, 7)
    sz_in()
    total = fold[pl.ds(pl.multiple_of(zh * PAD, PAD), PAD), :]
    for d in range(1, 4):
        total = total + fold_recv[d]
    out_ref[...] = total[:seqs, :]

    @pl.when(native)
    def _():
        for m in range(2):
            for s in range(2):
                z_copy(m, s, place(zl, y, m, beside, x), 1, m).wait_send()

                @pl.when(core != m)
                def _():
                    z_copy(m, s, sibling, 0, 2).wait_send()

        pin_remote.wait_send()

        @pl.when(next_to_across)
        def _():
            for s in range(2):
                quarter_out(s).wait_send()

    @pl.when(foreign)
    def _():
        for s in range(2):
            for m in range(2):
                z_copy(m, s, place(zl, y, m, across, x), 2, m).wait_send()

            @pl.when(next_to_across)
            def _():
                quarter_on(s).wait_send()

            quarter_up(s).wait_send()
            quarter_down(s).wait_send()
        half_up.wait_send()
        half_down.wait_send()
        left_copy(0).wait_send()

    for s in range(2):
        z_forward(s).wait_send()
    for j in range(4):
        for k in range(6):
            x_copy(j, k).wait_send()
        for k in range(4):
            sib_copy(j, k).wait_send()

    def left_done(d, carry):
        left_copy(d).wait_send()
        return carry

    lax.fori_loop(1, N, left_done, 0)
    for sent in (right_sent, rall_sent, gz_sent, gx_sent, part_sent, pall_sent, sx_sent, sz_sent):
        sent()


def body(inputs, cotangent, gate_weight, up_weight, proj_in, proj_out, inverse_fisher, stored):
    tokens, width = inputs.shape
    units = gate_weight.shape[1]
    feats, wide = inverse_fisher.shape
    rows = N * PAD
    f32, bf16 = jnp.float32, jnp.bfloat16
    dma = pltpu.SemaphoreType.DMA
    return pl.pallas_call(
        scores_kernel,
        out_shape=jax.ShapeDtypeStruct((tokens // TOK_SEQ, stored.shape[0]), f32),
        in_specs=[pl.BlockSpec(memory_space=pl.ANY)] * 8,
        out_specs=pl.BlockSpec(memory_space=pltpu.VMEM),
        scratch_shapes=[
            pltpu.VMEM((2, width, units), bf16),
            pltpu.VMEM((tokens, width), bf16),
            pltpu.VMEM((tokens, units), f32),
            pltpu.VMEM((tokens, units), f32),
            pltpu.VMEM((units, KIN), bf16),
            pltpu.VMEM(cotangent.shape, bf16),
            pltpu.VMEM(proj_out.shape, bf16),
            pltpu.VMEM(inverse_fisher.shape, bf16),
            pltpu.VMEM(stored.shape, bf16),
            pltpu.VMEM((KIN, tokens), f32),
            pltpu.VMEM((N, 8, tokens), f32),
            pltpu.VMEM((tokens, KOUT), f32),
            pltpu.VMEM((N, tokens // N, KOUT), f32),
            pltpu.VMEM((tokens // N, KOUT), f32),
            pltpu.VMEM((tokens, KOUT), f32),
            pltpu.VMEM((rows, feats), bf16),
            pltpu.VMEM((rows, wide), bf16),
            pltpu.VMEM((N, PAD, wide), bf16),
            pltpu.VMEM((PAD, wide), bf16),
            pltpu.VMEM((rows, wide), bf16),
            pltpu.VMEM((rows, stored.shape[0]), bf16),
            pltpu.VMEM((4, 4 * PAD, stored.shape[0]), bf16),
            pltpu.VMEM((4 * PAD, stored.shape[0]), f32),
            pltpu.VMEM((4, PAD, stored.shape[0]), f32),
            dma((7,)),
            dma((4, 2)), dma((4, 2)),
            dma((4, 6)), dma((4, 6)),
            dma((4, 4)), dma((4, 4)),
            dma((11,)), dma((11,)),
            dma((7, N)), dma((7, N)),
        ],
        compiler_params=pltpu.CompilerParams(
            collective_id=1, has_side_effects=True, vmem_limit_bytes=60 * 1024 * 1024),
        name="scores",
    )(inputs, cotangent, gate_weight, up_weight, proj_in, proj_out, inverse_fisher, stored)


def solution(mesh):
    return jax.shard_map(
        body,
        mesh=mesh,
        in_specs=(
            P("col", None),
            P("col", "row"),
            P("col", "row"),
            P("col", "row"),
            P("row", None),
            P("row", None),
            P("row", "col"),
            P("row", "col"),
        ),
        out_specs=P("col", "row"),
        check_vma=False,
    )
```

time: 550 us -> 162 us (0.29)
  waiting for transfers between devices: 328 us -> 0 us
  Pallas kernels: 0 us -> 159 us
  blocking collectives: 157 us -> 0 us
  matrix products: 32.9 us -> 0 us
  between operations: 13.9 us -> 0.01 us
  starting transfers between devices: 13.3 us -> 0 us
    all_gather x2 -> x0, waiting for transfers between devices: 195 us -> none  [the longest x1 99 us: body(): lax.all_gather(gate_weight, 'col', axis=0, tiled=True)]
    pallas_call x0 -> x1, Pallas kernels: none -> 159 us  [body(): pl.pallas_call(scores_kernel, out_shape=jax.ShapeDtypeStruct((tokens // T...]
    psum x1 -> x0, waiting for transfers between devices: 130 us -> none  [body(): left_proj, right_proj = lax.psum((left_part, right_part), 'row')]
    psum x1 -> x0, blocking collectives: 61.7 us -> none  [body(): precond = lax.psum(precond_part, 'row').astype(jnp.bfloat16)]
    unnamed x1 -> x0, blocking collectives: 49.3 us -> none
    all_gather x1 -> x0, blocking collectives: 46.5 us -> none  [body(): lax.all_gather(block_grads.astype(jnp.bfloat16), 'col', axis=0, tiled=True)]
    dot_general x6 -> x0, matrix products: 32.9 us -> none  [the longest x1 13.4 us: body(): left_part = jnp.dot(hidden, proj_in, preferred_element_type=jnp.float32)]
    unnamed x4 -> x0, starting transfers between devices: 13.2 us -> none
  transfers between devices with their start and end apart: 7 -> 0, of which waited for: 4 -> 0; matrix products, arithmetic and copies ran while one was open for 3% -> 0% of each run, Pallas kernels for 0% -> 0%
where the time goes in v3:
time: 162 us; the launch traced here: 160 us
  Pallas kernels  159 us (98%)
    pallas_call x1, Pallas kernels, body(): pl.pallas_call(scores_kernel, out_shape=jax.ShapeDtypeStruct((tokens // T...  159 us

profile of v3, /device:TPU:24, one launch (start us, length us, event | category | flops | bytes accessed | tf_op | source)
XLA Modules:
  0.0 160.4 jit_solution(525466386406790145)
XLA Ops:
  0.0 158.9 %scores.1 = f32[12,1024]{1,0:T(8,128)} custom-call(bf16[768,4096]{1,0:T(8,128)(2,1)} %x_hbm.1, bf16[768,256]{1,0:T(8,128)(2,1)} %cot_hbm.1, bf16[256,896]{1,0:T(8,128)(2,1)} %gate_hbm.1, bf16[256,896]{1,0:T(8,128)(2,1)} %up_hbm.1, bf16[896,128]{1,0:T(8,128)(2,1)} %pin_hbm.1, bf16[256,128]{1,0:T(8,128)(2,1)} %pout_hbm.1, bf16[1024,1024]{1,0:T(8,128)(2,1)} %fisher_hbm.1, ...), custom_call_target="tpu_custom_call" | custom-call | tf_op jit(solution)/shard_map/scores/pallas_call | solution.py:503
  158.9 1.5 copy.10

commit v4 on v3

--- a/solution.py
+++ b/solution.py
@@ -26,7 +26,7 @@
     x_hbm, cot_hbm, gate_hbm, up_hbm, pin_hbm, pout_hbm, fisher_hbm, stored_hbm, out_ref,
     weights, acts, acc_gate, acc_up, pin, cot, pout, fisher, stored,
     left_part, left_recv, right_part, right_recv, right_own, right_all,
-    grads_all, part, part_recv, prec_own, prec_all, part2, part2_recv, fold, fold_recv,
+    grads_all, packed, part, part_recv, prec_own, prec_all, part2, part2_recv, fold, fold_recv,
     local_sem, z_send, z_recv, x_send, x_recv, sib_send, sib_recv, in_send, in_recv,
     tail_send, tail_recv,
 ):
@@ -56,9 +56,11 @@
     group = 4 * depth
     tokens = x_hbm.shape[0]
     quarter = tokens // 4
-    eighth = quarter // 2
+    slab = quarter // 4
     tok_blk = tokens // N
     seqs = tokens // TOK_SEQ
+    high = 4 * seqs
+    broad = fisher.shape[1] // 4
     sibling = place(zl, y, 1 - core, zh, x)
     token_col = jnp.where(native, zh, across) * 4 + x
 
@@ -75,11 +77,13 @@
     for load in loads:
         load.start()
 
+    fold[...] = jnp.zeros_like(fold)
     barrier = pltpu.get_barrier_semaphore()
-    partners = [row_dev(d) for d in range(1, N)]
-    partners += [{"row": lax.rem(row + d, N), "col": across * 4 + x} for d in range(N)]
-    partners += [place(zl, y, 0, beside, x), place(zl, y, 1, beside, x), place(zl, y, core, across_beside, x)]
-    partners += [place(zl, y, core, zh, side) for side in (right, left, far)]
+    partners = [{"row": lax.rem(row + d, N), "col": across * 4 + x} for d in range(N)]
+    partners += [place(zl, y, core, across_beside, x)]
+    partners += [place(zl, y, core, zh, side) for side in (far, right, left)]
+    partners += [place(zl, y, 0, beside, x), place(zl, y, 1, beside, x)]
+    partners += [row_dev(d) for d in range(1, N)]
     for partner in partners:
         pl.semaphore_signal(barrier, inc=1, device_id=partner)
     pl.semaphore_wait(barrier, len(partners))
@@ -102,7 +106,7 @@
         return remote(ref, ref, z_send.at[3, s], z_recv.at[j, s], sibling)
 
     def in_copy(src_ref, q, s, slot, recv_slot, device):
-        at = pl.ds(q * quarter + s * eighth, eighth)
+        at = pl.ds(q * quarter + s * slab, slab)
         return remote(src_ref.at[at], acts.at[at], in_send.at[slot], in_recv.at[recv_slot], device)
 
     pin_remote = remote(pin_hbm, pin, in_send.at[0], in_recv.at[0], sibling)
@@ -111,16 +115,18 @@
         return in_copy(x_hbm, y, s, 1 + s, 1 + s, place(1 - zl, y, core, across, x))
 
     def quarter_on(s):
-        return in_copy(acts, y, s, 3 + s, 1 + s, place(1 - zl, y, core, zh, x))
+        return in_copy(acts, y, s, 5 + s, 1 + s, place(1 - zl, y, core, zh, x))
 
     def quarter_up(s):
-        return in_copy(acts, y, s, 5 + s, 5 + s, place(zl, up_y, core, zh, x))
+        return in_copy(acts, y, s, 9 + s, 9 + s, place(zl, up_y, core, zh, x))
 
     def quarter_down(s):
-        return in_copy(acts, y, s, 7 + s, 7 + s, place(zl, down_y, core, zh, x))
-
-    half_up = in_copy(acts, down_y, 0, 9, 9, place(zl, up_y, core, zh, x))
-    half_down = in_copy(acts, up_y, 1, 10, 10, place(zl, down_y, core, zh, x))
+        return in_copy(acts, y, s, 13 + s, 13 + s, place(zl, down_y, core, zh, x))
+
+    def far_quarter(s):
+        if s < 2:
+            return in_copy(acts, down_y, s, 17 + s, 17 + s, place(zl, up_y, core, zh, x))
+        return in_copy(acts, up_y, s, 17 + s, 17 + s, place(zl, down_y, core, zh, x))
 
     def own_copy(m):
         return pltpu.make_async_copy(mats[m], block(m, zh, x), local_sem.at[6])
@@ -140,7 +146,7 @@
 
         @pl.when(next_to_across)
         def _():
-            for s in range(2):
+            for s in range(4):
                 quarter_out(s).start()
 
         for s in range(2):
@@ -218,27 +224,28 @@
             quarter_up(s).start()
             quarter_down(s).start()
 
-    def pass_quarters():
+    def pass_quarter(s):
         @pl.when(foreign)
         def _():
-            quarter_up(0).wait_recv()
-            half_up.start()
-            quarter_up(1).wait_recv()
-            quarter_down(0).wait_recv()
-            quarter_down(1).wait_recv()
-            half_down.start()
+            quarter_up(s).wait_recv()
+            quarter_down(s).wait_recv()
+            far_quarter(s).start()
 
     def have_inputs():
         @pl.when(foreign)
         def _():
-            half_up.wait_recv()
-            half_down.wait_recv()
+            for s in range(4):
+                far_quarter(s).wait_recv()
             pin_remote.wait_recv()
 
         @pl.when(native)
         def _():
+            pin_copy.wait()
+
+    def own_kind():
+        @pl.when(native)
+        def _():
             acts_copy.wait()
-            pin_copy.wait()
 
     def many(phase, src_of, dst_of, dev_of, first=1, last=N):
         def copy(d):
@@ -257,11 +264,17 @@
     def at_row(d):
         return lax.rem(row + d, N)
 
-    def deep_dot(j, rows, start=0, size=group):
-        deep = pl.ds(pl.multiple_of(sources[j] * group + start, 256), size)
+    def deep_dot(rows, start, size):
+        deep = pl.ds(pl.multiple_of(start, 256), size)
         a = acts[rows, deep]
         return (jnp.dot(a, weights[0, deep, :], preferred_element_type=jnp.float32),
                 jnp.dot(a, weights[1, deep, :], preferred_element_type=jnp.float32))
+
+    def group_dot(j, rows):
+        return deep_dot(rows, sources[j] * group, group)
+
+    def piece_dot(j, k, rows):
+        return deep_dot(rows, sources[j] * group + sides[k] * depth, depth)
 
     def tiles(step):
         def at(t, carry):
@@ -270,24 +283,51 @@
 
         lax.fori_loop(0, tokens // TILE, at, 0)
 
-    def compute_first():
-        def step(rows):
-            gate, up = deep_dot(0, rows)
-            acc_gate[rows, :] = gate
-            acc_up[rows, :] = up
-
-        tiles(step)
+    def quarter_rows(ahead):
+        return pl.ds(pl.multiple_of(lax.rem(y + ahead, 4) * quarter, 64), quarter)
+
+    def compute_near(j):
+        def step(t, carry):
+            rows = quarter_rows(t + t // 2)
+            gate, up = group_dot(j, rows)
+            if j == 0:
+                acc_gate[rows, :] = gate
+                acc_up[rows, :] = up
+            else:
+                acc_gate[rows, :] += gate
+                acc_up[rows, :] += up
+            return carry
+
+        lax.fori_loop(0, 3, step, 0)
+
+    def compute_last():
+        rows = quarter_rows(2)
+        gate0, up0 = group_dot(0, rows)
+        gate1, up1 = group_dot(1, rows)
+        acc_gate[rows, :] = gate0 + gate1
+        acc_up[rows, :] = up0 + up1
 
     def compute_add(j):
         def step(rows):
-            gate, up = deep_dot(j, rows)
+            gate, up = group_dot(j, rows)
             acc_gate[rows, :] += gate
             acc_up[rows, :] += up
 
         tiles(step)
 
-    def sibs(j):
-        for k in range(4):
+    def compute_pieces(j):
+        def step(rows):
+            for m, acc in ((0, acc_gate), (1, acc_up)):
+                total = acc[rows, :]
+                for k in range(3):
+                    deep = pl.ds(pl.multiple_of(sources[j] * group + sides[k] * depth, 256), depth)
+                    total = total + jnp.dot(acts[rows, deep], weights[m, deep, :], preferred_element_type=jnp.float32)
+                acc[rows, :] = total
+
+        tiles(step)
+
+    def sibs(j, first=0, last=4):
+        for k in range(first, last):
             sib_arrival(j, k)
 
     have_column(0, 0)
@@ -301,17 +341,20 @@
     have_side(0, 0)
     across_start(0)
     have_quarter(0)
-    have_column(1, 0)
     have_side(0, 1)
     across_start(1)
+    have_column(1, 0)
     have_quarter(1)
+    have_far(0)
     have_column(1, 1)
-    have_far(0)
+    have_quarter(2)
+    pass_quarter(0)
     have_column(2, 0)
     have_side(1, 0)
+    have_quarter(3)
+    pass_quarter(1)
     have_side(1, 1)
     have_column(2, 1)
-
     right_in()
     total = right_part[pl.ds(row * tok_blk, tok_blk), :]
     for d in range(1, N):
@@ -322,27 +365,32 @@
         2, lambda d: right_own,
         lambda d: right_all.at[pl.ds(row * tok_blk, tok_blk)], row_dev)
 
+    pass_quarter(2)
+    have_far(1)
     have_column(3, 0)
-    pass_quarters()
-    have_far(1)
+    pass_quarter(3)
     have_side(2, 0)
+    have_column(3, 1)
     have_side(2, 1)
-    have_column(3, 1)
+    own_kind()
+    sibs(0)
+    compute_near(0)
+    sibs(1)
+    compute_near(1)
     have_inputs()
-    sibs(0)
-    compute_first()
+    compute_last()
     have_far(2)
     have_side(3, 0)
-    have_side(3, 1)
-    sibs(1)
-    compute_add(1)
     sibs(2)
     compute_add(2)
+    have_side(3, 1)
+    sibs(3, 0, 3)
+    compute_pieces(3)
     have_far(3)
-    sibs(3)
+    sibs(3, 3, 4)
 
     def finish(rows):
-        gate, up = deep_dot(3, rows)
+        gate, up = piece_dot(3, 3, rows)
         gate = acc_gate[rows, :] + gate
         up = acc_up[rows, :] + up
         hidden = (gate / (1.0 + jnp.exp(-gate)) * up).astype(jnp.bfloat16)
@@ -392,7 +440,6 @@
         [jnp.where(inside, jnp.broadcast_to(total[i : i + 1, :], (PAD, tokens)), 0.0) for i in range(8)], axis=0)
     grads = jnp.dot(spread, right_all[...], preferred_element_type=jnp.float32, precision=lax.Precision.HIGHEST)
     mine = pl.ds(pl.multiple_of((x * 4 + zh) * PAD, PAD), PAD)
-    column = pl.ds(pl.multiple_of(x * 4 * PAD, PAD), 4 * PAD)
     for i in range(8):
         grads_all[mine, i * KOUT : (i + 1) * KOUT] = grads[i * PAD : (i + 1) * PAD, :].astype(jnp.bfloat16)
 
@@ -402,46 +449,81 @@
     def x_dev(d):
         return place(zl, y, core, zh, lax.rem(x + d, 4))
 
-    gz_in, gz_sent = many(3, lambda d: grads_all.at[mine], lambda d: grads_all.at[mine], z_dev, 1, 4)
-    gz_in()
-    gx_in, gx_sent = many(
-        3, lambda d: grads_all.at[column], lambda d: grads_all.at[column], lambda d: x_dev(d - 3), 4, 7)
+    def grads_z(d):
+        return remote(grads_all.at[mine], grads_all.at[mine], tail_send.at[3, d], tail_recv.at[3, d], z_dev(d))
+
+    def grads_x(d, e):
+        at = grads_all.at[pl.ds((x * 4 + lax.rem(zh + 4 - d, 4)) * PAD, PAD)]
+        return remote(at, at, tail_send.at[7, d * 3 + e - 1], tail_recv.at[7, d * 3 + e - 1], x_dev(e))
+
+    for d in (2, 1, 3):
+        grads_z(d).start()
+    for d in (0, 1, 3, 2):
+        if d > 0:
+            grads_z(d).wait_recv()
+        for e in (2, 1, 3):
+            grads_x(d, e).start()
     loads[2].wait()
-    gx_in()
-    part[...] = jnp.dot(
-        grads_all[...], fisher[...], preferred_element_type=jnp.float32).astype(jnp.bfloat16)
-    part_in, part_sent = many(
-        4, lambda d: part.at[pl.ds(at_row(d) * PAD, PAD)],
-        lambda d: part_recv.at[d], row_dev)
-    row_rows = pl.ds(pl.multiple_of(row * PAD, PAD), PAD)
+    for d in (0, 1, 3, 2):
+        for e in (1, 3, 2):
+            grads_x(d, e).wait_recv()
+    padded = jnp.dot(grads_all[...], fisher[...], preferred_element_type=jnp.float32)
+    for b in range(N):
+        packed[b * seqs : (b + 1) * seqs, :] = padded[b * PAD : b * PAD + seqs, :]
+    part[...] = packed[...].astype(jnp.bfloat16)
+
+    def piece(r):
+        return (pl.ds(pl.multiple_of(r // 4 * high, high), high), pl.ds(pl.multiple_of(lax.rem(r, 4) * broad, broad), broad))
+
+    part_in, part_sent = many(4, lambda d: part.at[piece(at_row(d))], lambda d: part_recv.at[d], row_dev)
     part_in()
-    total = part[row_rows, :].astype(jnp.float32)
+    total = part[piece(row)].astype(jnp.float32)
     for d in range(1, N):
         total = total + part_recv[d].astype(jnp.float32)
     prec_own[...] = total.astype(jnp.bfloat16)
-    prec_all[row_rows, :] = total.astype(jnp.bfloat16)
-    pall_in, pall_sent = many(
-        5, lambda d: prec_own, lambda d: prec_all.at[pl.ds(row * PAD, PAD)], row_dev)
+    prec_all[piece(row)] = total.astype(jnp.bfloat16)
+    pall_in, pall_sent = many(5, lambda d: prec_own, lambda d: prec_all.at[piece(row)], row_dev)
     loads[3].wait()
     pall_in()
-    part2[...] = lax.dot_general(
-        prec_all[...], stored[...], (((1,), (1,)), ((), ())), preferred_element_type=jnp.float32).astype(jnp.bfloat16)
-    sx_in, sx_sent = many(
-        6, lambda d: part2.at[pl.ds(lax.rem(x + d, 4) * 4 * PAD, 4 * PAD)],
-        lambda d: part2_recv.at[d], x_dev, 1, 4)
-    sx_in()
-    total = part2[column, :].astype(jnp.float32)
-    for d in range(1, 4):
-        total = total + part2_recv[d].astype(jnp.float32)
-    fold[...] = total
-    sz_in, sz_sent = many(
-        6, lambda d: fold.at[pl.ds(lax.rem(zh + d - 3, 4) * PAD, PAD)],
-        lambda d: fold_recv.at[d - 3], lambda d: z_dev(d - 3), 4, 7)
-    sz_in()
-    total = fold[pl.ds(pl.multiple_of(zh * PAD, PAD), PAD), :]
-    for d in range(1, 4):
-        total = total + fold_recv[d]
-    out_ref[...] = total[:seqs, :]
+    span = stored.shape[0] // 2
+    column = pl.ds(pl.multiple_of(x * high, high), high)
+
+    def sum_x(h, d):
+        return remote(
+            part2.at[pl.ds(lax.rem(x + d, 4) * high, high), pl.ds(h * span, span)],
+            part2_recv.at[d, :, pl.ds(h * span, span)],
+            tail_send.at[6, h * 8 + d], tail_recv.at[6, h * 8 + d], x_dev(d))
+
+    def sum_z(h, d):
+        return remote(
+            fold.at[lax.rem(zh + d, 4), :, pl.ds(h * span, span)],
+            fold_recv.at[d, :, pl.ds(h * span, span)],
+            tail_send.at[6, h * 8 + 4 + d], tail_recv.at[6, h * 8 + 4 + d], z_dev(d))
+
+    for h in range(2):
+        cols = slice(h * span, (h + 1) * span)
+        part2[:, cols] = lax.dot_general(
+            prec_all[...], stored[cols, :], (((1,), (1,)), ((), ())),
+            preferred_element_type=jnp.float32).astype(jnp.bfloat16)
+        for d in (2, 1, 3):
+            sum_x(h, d).start()
+    for h in range(2):
+        cols = slice(h * span, (h + 1) * span)
+        total = part2[column, cols].astype(jnp.float32)
+        for d in (1, 3, 2):
+            sum_x(h, d).wait_recv()
+            total = total + part2_recv[d, :, cols].astype(jnp.float32)
+        for b in range(4):
+            fold[b, :seqs, cols] = total[b * seqs : (b + 1) * seqs, :]
+        for d in (2, 1, 3):
+            sum_z(h, d).start()
+    for h in range(2):
+        cols = slice(h * span, (h + 1) * span)
+        total = fold[zh, :, cols]
+        for d in (1, 3, 2):
+            sum_z(h, d).wait_recv()
+            total = total + fold_recv[d, :, cols]
+        out_ref[:, cols] = total[:seqs, :]
 
     @pl.when(native)
     def _():
@@ -457,7 +539,7 @@
 
         @pl.when(next_to_across)
         def _():
-            for s in range(2):
+            for s in range(4):
                 quarter_out(s).wait_send()
 
     @pl.when(foreign)
@@ -465,6 +547,7 @@
         for s in range(2):
             for m in range(2):
                 z_copy(m, s, place(zl, y, m, across, x), 2, m).wait_send()
+        for s in range(4):
 
             @pl.when(next_to_across)
             def _():
@@ -472,8 +555,7 @@
 
             quarter_up(s).wait_send()
             quarter_down(s).wait_send()
-        half_up.wait_send()
-        half_down.wait_send()
+            far_quarter(s).wait_send()
         left_copy(0).wait_send()
 
     for s in range(2):
@@ -489,7 +571,15 @@
         return carry
 
     lax.fori_loop(1, N, left_done, 0)
-    for sent in (right_sent, rall_sent, gz_sent, gx_sent, part_sent, pall_sent, sx_sent, sz_sent):
+    for d in range(1, 4):
+        grads_z(d).wait_send()
+        for h in range(2):
+            sum_x(h, d).wait_send()
+            sum_z(h, d).wait_send()
+    for d in range(4):
+        for e in range(1, 4):
+            grads_x(d, e).wait_send()
+    for sent in (right_sent, rall_sent, part_sent, pall_sent):
         sent()
 
 
@@ -497,7 +587,7 @@
     tokens, width = inputs.shape
     units = gate_weight.shape[1]
     feats, wide = inverse_fisher.shape
-    rows = N * PAD
+    rows = N * (tokens // TOK_SEQ)
     f32, bf16 = jnp.float32, jnp.bfloat16
     dma = pltpu.SemaphoreType.DMA
     return pl.pallas_call(
@@ -521,21 +611,22 @@
             pltpu.VMEM((N, tokens // N, KOUT), f32),
             pltpu.VMEM((tokens // N, KOUT), f32),
             pltpu.VMEM((tokens, KOUT), f32),
-            pltpu.VMEM((rows, feats), bf16),
+            pltpu.VMEM((N * PAD, feats), bf16),
+            pltpu.VMEM((rows, wide), f32),
             pltpu.VMEM((rows, wide), bf16),
-            pltpu.VMEM((N, PAD, wide), bf16),
-            pltpu.VMEM((PAD, wide), bf16),
+            pltpu.VMEM((N, rows // 4, wide // 4), bf16),
+            pltpu.VMEM((rows // 4, wide // 4), bf16),
             pltpu.VMEM((rows, wide), bf16),
             pltpu.VMEM((rows, stored.shape[0]), bf16),
-            pltpu.VMEM((4, 4 * PAD, stored.shape[0]), bf16),
-            pltpu.VMEM((4 * PAD, stored.shape[0]), f32),
+            pltpu.VMEM((4, rows // 4, stored.shape[0]), bf16),
+            pltpu.VMEM((4, PAD, stored.shape[0]), f32),
             pltpu.VMEM((4, PAD, stored.shape[0]), f32),
             dma((7,)),
             dma((4, 2)), dma((4, 2)),
             dma((4, 6)), dma((4, 6)),
             dma((4, 4)), dma((4, 4)),
-            dma((11,)), dma((11,)),
-            dma((7, N)), dma((7, N)),
+            dma((21,)), dma((21,)),
+            dma((8, N)), dma((8, N)),
         ],
         compiler_params=pltpu.CompilerParams(
             collective_id=1, has_side_effects=True, vmem_limit_bytes=60 * 1024 * 1024),

time: 162 us -> 151 us (0.932)
  Pallas kernels: 159 us -> 149 us
    pallas_call x1, Pallas kernels: 159 us -> 149 us  [body(): pl.pallas_call(scores_kernel, out_shape=jax.ShapeDtypeStruct((tokens // T...]
where the time goes in v4:
time: 151 us; the launch traced here: 150 us
  Pallas kernels  149 us (99%)
    pallas_call x1, Pallas kernels, body(): pl.pallas_call(scores_kernel, out_shape=jax.ShapeDtypeStruct((tokens // T...  149 us

profile of v4, /device:TPU:24, one launch (start us, length us, event | category | flops | bytes accessed | tf_op | source)
XLA Modules:
  0.0 150.1 jit_solution(8412257998787882539)
XLA Ops:
  0.0 148.6 %scores.1 = f32[12,1024]{1,0:T(8,128)} custom-call(bf16[768,4096]{1,0:T(8,128)(2,1)} %x_hbm.1, bf16[768,256]{1,0:T(8,128)(2,1)} %cot_hbm.1, bf16[256,896]{1,0:T(8,128)(2,1)} %gate_hbm.1, bf16[256,896]{1,0:T(8,128)(2,1)} %up_hbm.1, bf16[896,128]{1,0:T(8,128)(2,1)} %pin_hbm.1, bf16[256,128]{1,0:T(8,128)(2,1)} %pout_hbm.1, bf16[1024,1024]{1,0:T(8,128)(2,1)} %fisher_hbm.1, ...), custom_call_target="tpu_custom_call" | custom-call | tf_op jit(solution)/shard_map/scores/pallas_call | solution.py:593
  148.6 1.5 copy.10

commit v5 on v4

--- a/solution.py
+++ b/solution.py
@@ -375,15 +375,15 @@
     own_kind()
     sibs(0)
     compute_near(0)
+    have_side(3, 0)
     sibs(1)
     compute_near(1)
+    have_side(3, 1)
+    have_far(2)
     have_inputs()
     compute_last()
-    have_far(2)
-    have_side(3, 0)
     sibs(2)
     compute_add(2)
-    have_side(3, 1)
     sibs(3, 0, 3)
     compute_pieces(3)
     have_far(3)

time: 151 us -> 148 us (0.980)
  Pallas kernels: 149 us -> 147 us
    pallas_call x1, Pallas kernels: 149 us -> 147 us  [body(): pl.pallas_call(scores_kernel, out_shape=jax.ShapeDtypeStruct((tokens // T...]
where the time goes in v5:
time: 148 us
  Pallas kernels  147 us (99%)
    pallas_call x1, Pallas kernels, body(): pl.pallas_call(scores_kernel, out_shape=jax.ShapeDtypeStruct((tokens // T...  147 us

profile of v5, /device:TPU:24, one launch (start us, length us, event | category | flops | bytes accessed | tf_op | source)
XLA Modules:
  0.0 148.1 jit_solution(7400727900844647473)
XLA Ops:
  0.0 146.6 %scores.1 = f32[12,1024]{1,0:T(8,128)} custom-call(bf16[768,4096]{1,0:T(8,128)(2,1)} %x_hbm.1, bf16[768,256]{1,0:T(8,128)(2,1)} %cot_hbm.1, bf16[256,896]{1,0:T(8,128)(2,1)} %gate_hbm.1, bf16[256,896]{1,0:T(8,128)(2,1)} %up_hbm.1, bf16[896,128]{1,0:T(8,128)(2,1)} %pin_hbm.1, bf16[256,128]{1,0:T(8,128)(2,1)} %pout_hbm.1, bf16[1024,1024]{1,0:T(8,128)(2,1)} %fisher_hbm.1, ...), custom_call_target="tpu_custom_call" | custom-call | tf_op jit(solution)/shard_map/scores/pallas_call | solution.py:593
  146.7 1.5 copy.10

commit v6 on v5

--- a/solution.py
+++ b/solution.py
@@ -10,7 +10,7 @@
 TOK_SEQ = 64
 N = 16
 PAD = 16
-TILE = 256
+TILE = 384
 
 
 def place(zl, y, core, zh, x):

time: 148 us -> 148 us (level)
  no operation moved by 1% of the time
where the time goes in v6:
time: 148 us; the launch traced here: 147 us
  Pallas kernels  146 us (99%)
    pallas_call x1, Pallas kernels, body(): pl.pallas_call(scores_kernel, out_shape=jax.ShapeDtypeStruct((tokens // T...  146 us

profile of v6, /device:TPU:24, one launch (start us, length us, event | category | flops | bytes accessed | tf_op | source)
XLA Modules:
  0.0 147.4 jit_solution(708708159933337830)
XLA Ops:
  0.0 146.0 %scores.1 = f32[12,1024]{1,0:T(8,128)} custom-call(bf16[768,4096]{1,0:T(8,128)(2,1)} %x_hbm.1, bf16[768,256]{1,0:T(8,128)(2,1)} %cot_hbm.1, bf16[256,896]{1,0:T(8,128)(2,1)} %gate_hbm.1, bf16[256,896]{1,0:T(8,128)(2,1)} %up_hbm.1, bf16[896,128]{1,0:T(8,128)(2,1)} %pin_hbm.1, bf16[256,128]{1,0:T(8,128)(2,1)} %pout_hbm.1, bf16[1024,1024]{1,0:T(8,128)(2,1)} %fisher_hbm.1, ...), custom_call_target="tpu_custom_call" | custom-call | tf_op jit(solution)/shard_map/scores/pallas_call | solution.py:593
  146.0 1.5 copy.10
